TPU v7x, 32 devices: a whole 2x2x4 slice. The times are simulated.
32 devices in a mesh: row: 4 (over z), col: 8 (over y, x, core).
Axes of the slice: x: 2, y: 2, z: 4, core: 2. Of those that a mesh axis runs over, the one named last changes fastest.
Arguments:
- joined_weight: bfloat16 [8, 2880, 5760], P('row', 'col'), may hold values from -0.109375 to 0.109375
- tile_perm: int32 [144], replicated, may hold values from 0 to 143, each once
- down_weight: bfloat16 [8, 2880, 2880], P('row', 'col'), may hold values from -0.109375 to 0.109375
- tokens: bfloat16 [256, 2880], P(('row', 'col')), may hold values from -6 to 6
- expert_ids: int32 [256, 4], replicated, may hold values from 0 to 7, all different within a row; in each aligned block of 256 rows (0 to 255, 256 to 511, ...) at most 256 rows name the same one
- route_scores: float32 [256, 4], replicated, may hold values from 0.1 to 1
Outputs:
- gate_weight: bfloat16 [8, 2880, 2880], P('row', None, 'col')
- up_weight: bfloat16 [8, 2880, 2880], P('row', None, 'col')
- mixed: bfloat16 [256, 2880], P(('row', 'col'))
Inputs may be any that keep to these rules, and one draw needn't show every extreme that they name: `expert_ids`: every expert is chosen by at most 256 tokens, a bound that some block reaches.
All inputs are finite; a program needn't handle non-finite values.
Results may differ from a plain program's by a relative error of at most 0.0049.
Values may be sent and summed in bfloat16 or wider, within the bound.
A program may use at most 128 MiB of HBM per device.

v0:
```python
import jax
import jax.numpy as jnp
from jax import lax
from jax.sharding import PartitionSpec as P


def body(joined_weight, tile_perm, down_weight, tokens, expert_ids, route_scores):
    n_col = lax.axis_size("col")
    local = joined_weight.shape[0]
    width = joined_weight.shape[2]
    ff_local = width // 2 // n_col
    tiles = tile_perm.shape[0]
    tile_cols = width // tiles
    places = jnp.arange(tiles, dtype=jnp.int32)
    inverse = jnp.sum(places[:, None] * (tile_perm[:, None] == places[None, :]), axis=0)
    order = jnp.arange(width, dtype=jnp.int32)
    block = order // (2 * ff_local)
    within = order % (2 * ff_local)
    logical = 2 * (block * ff_local + within % ff_local) + within // ff_local
    lookup = (logical // tile_cols)[:, None] == places[None, :]
    stored = jnp.sum(lookup * inverse[None, :], axis=1) * tile_cols + logical % tile_cols
    packed = jnp.take(joined_weight, stored, axis=2)
    everything = lax.all_gather(tokens, ("row", "col"), axis=0, tiled=True)
    expert_global = lax.axis_index("row") * local + jnp.arange(local, dtype=jnp.int32)
    weights = route_scores / jnp.sum(route_scores, axis=1, keepdims=True)
    share = jnp.sum(
        weights[:, :, None] * (expert_ids[:, :, None] == expert_global[None, None, :]), axis=1
    )
    weights_in = lax.all_to_all(packed, "col", split_axis=2, concat_axis=1, tiled=True)
    gate_part = weights_in[:, :, :ff_local]
    up_part = weights_in[:, :, ff_local:]
    pre_gate = jnp.einsum("td,ndf->ntf", everything, gate_part, preferred_element_type=jnp.float32)
    pre_up = jnp.einsum("td,ndf->ntf", everything, up_part, preferred_element_type=jnp.float32)
    gate_out, up_out = (gate_part, up_part)
    pre_gate, pre_up = (pre_gate, pre_up)
    active = share.T[:, :, None] * (pre_up + 1.0) * pre_gate * jax.nn.sigmoid(1.702 * pre_gate)
    active = active.astype(jnp.bfloat16)
    total = lax.psum_scatter(
        jnp.einsum("ntf,nfd->td", active, down_weight, preferred_element_type=jnp.float32),
        ("row", "col"),
        scatter_dimension=0,
        tiled=True,
    )
    return (gate_out, up_out, total.astype(jnp.bfloat16))


def solution(mesh):
    placed = (P("row", "col", None), P(), P("row", "col", None), P(("row", "col"), None), P(), P())
    return jax.shard_map(
        body,
        mesh=mesh,
        in_specs=placed,
        out_specs=(P("row", None, "col"), P("row", None, "col"), P(("row", "col"), None)),
        check_vma=False,
    )
```

profile of v0, /device:TPU:0, one launch (start us, length us, event | category | flops | bytes accessed | tf_op | source)
XLA Modules:
  0.0 329.6 jit_solution(3264672544590070876)
XLA Ops:
  7.2 0.1 add_select_fusion.1
  7.2 0.8 select_reduce_fusion.1
  8.0 0.6 select_reduce_fusion
  8.6 0.1 compare_and_fusion
  8.7 0.5 fusion.51
  9.2 23.6 %copy.20 = bf16[2,360,5760]{1,0,2:T(2,128)(2,1)} copy(bf16[2,360,5760]{2,1,0:T(8,128)(2,1)} %param.6) | data formatting | bytes 16588800 | tf_op args[0]
  32.7 32.0 %gather_fusion = bf16[5760,2,360]{2,1,0:T(2,128)(2,1)} fusion(bf16[2,360,5760]{1,0,2:T(2,128)(2,1)} %copy.20, s32[6144]{0:T(1024)S(1)} %pad_clamp_fusion), kind=kCustom, calls=%fused_computation | custom fusion | bytes 16611840 | tf_op jit(solution)/shard_map/jit(_take)/gather | solution.py:22
  64.7 23.2 %fusion = bf16[2,360,5760]{1,0,2:T(2,128)(2,1)} fusion(bf16[5760,2,360]{2,1,0:T(2,128)(2,1)} %gather_fusion, pred[5760]{0:T(1024)(128)(4,1)S(1)} %compare_and_fusion), kind=kLoop, calls=%fused_computation.3 | loop fusion | flops 4147200 | bytes 16594560 | tf_op jit(solution)/shard_map/jit(_take)/select_n | solution.py:22
  87.9 0.0 copy-start
  87.9 0.0 copy-start.1
  87.9 5.3 %all-to-all-start = ((bf16[2,360,5760]{1,0,2:T(2,128)(2,1)}), bf16[2,360,5760]{1,0,2:T(2,128)(2,1)}, u32[]{:S(2)}, u32[]{:S(2)}) async-start(bf16[2,360,5760]{1,0,2:T(2,128)(2,1)} %fusion), calls=%async_computation | async-start | bytes 17694720 | tf_op jit(solution)/shard_map/all_to_all | solution.py:29
  93.2 0.2 all-gather.2.cloned.1.call-start
  93.4 0.5 all-gather.2.cloned.1.call-update
  93.9 0.0 copy-done
  94.0 0.0 copy-done.1
  94.0 0.1 select_reduce_fusion.2
  94.1 103.0 %all-to-all-done = bf16[2,360,5760]{1,0,2:T(2,128)(2,1)} async-done(((bf16[2,360,5760]{1,0,2:T(2,128)(2,1)}), bf16[2,360,5760]{1,0,2:T(2,128)(2,1)}, u32[]{:S(2)}, u32[]{:S(2)}) %all-to-all-start) | async-done | bytes 8294432 | tf_op jit(solution)/shard_map/all_to_all | solution.py:29
  197.0 10.2 %copy.23 = bf16[2,360,8,720]{1,2,3,0:T(8,128)(2,1)} copy(bf16[2,360,8,720]{1,0,3,2:T(2,128)(2,1)} %bitcast.1) | data formatting | bytes 16588800 | tf_op jit(solution)/shard_map/all_to_all | solution.py:29
  207.2 15.7 %all_to_all.16 = bf16[2,2880,720]{1,2,0:T(8,128)(2,1)} reshape(bf16[2,8,360,720]{2,1,3,0:T(8,128)(2,1)} %bitcast.39) | data formatting | bytes 16588800 | tf_op jit(solution)/shard_map/all_to_all | solution.py:29
  223.0 5.9 %fusion.57 = (bf16[2,2880,360]{1,2,0:T(8,128)(2,1)}, bf16[2,2880,360]{1,2,0:T(8,128)(2,1)}) fusion(bf16[2,2880,720]{1,2,0:T(8,128)(2,1)} %all_to_all.16), kind=kLoop, calls=%fused_computation.78 | loop fusion | bytes 16588800 | tf_op jit(solution)/shard_map/slice | solution.py:31
  228.9 0.0 all-gather.2.cloned.1.call-done
  228.9 4.9 %fusion.1 = f32[2,360,256]{2,1,0:T(8,128)} fusion(bf16[2,2880,360]{1,2,0:T(8,128)(2,1)} %get-tuple-element.4, bf16[256,2880]{1,0:T(8,128)(2,1)} %all-gather.2.cloned.1.call-done), kind=kOutput, calls=%fused_computation.7 | convolution fusion | flops 1061683200 | bytes 6359040 | tf_op jit(solution)/shard_map/td,ndf->ntf/dot_general | solution.py:32
  233.7 9.0 %convolution_bitcast_fusion = f32[256,2880]{1,0:T(8,128)S(1)} fusion(bf16[2,360,2880]{2,1,0:T(8,128)(2,1)} %param.8, f32[2,360,256]{2,1,0:T(8,128)} %fusion.1, bf16[2,2880,360]{1,2,0:T(8,128)(2,1)} %get-tuple-element.3, bf16[256,2880]{1,0:T(8,128)(2,1)} %all-gather.2.cloned.1.call-done, f32[2,256]{1,0:T(2,128)S(1)} %bitcast.40), kind=kOutput, calls=%fused_computation.4 | convolution fusion | flops 2125025280 | bytes 13457408 | tf_op jit(solution)/shard_map/ntf,nfd->td/dot_general | solution.py:39
  242.8 78.6 %all-reduce.2 = bf16[256,2880]{1,0:T(8,128)(2,1)} all-reduce(f32[256,2880]{1,0:T(8,128)S(1)} %convolution_bitcast_fusion), channel_id=2, replica_groups=mesh['row'=4,'col'=8] {'row','col'}, use_global_device_ids=true, to_apply=%region_4.5.clone | all-reduce | flops 737280 | bytes 4423680
  321.4 1.4 dynamic-slice_convert_fusion
  (5 shorter events, 0.0 us)
Async XLA Ops:
  87.9 6.1 %copy-start = (f32[256,4]{0,1:T(4,128)S(1)}, f32[256,4]{0,1:T(4,128)}, u32[]{:S(2)}) copy-start(f32[256,4]{0,1:T(4,128)} %param.11) | copy-start | bytes 12292
  87.9 6.1 %copy-start.1 = (s32[256,4]{0,1:T(4,128)S(1)}, s32[256,4]{0,1:T(4,128)}, u32[]{:S(2)}) copy-start(s32[256,4]{0,1:T(4,128)} %param.10) | copy-start | bytes 12292
  87.9 109.2 %all-to-all-start = ((bf16[2,360,5760]{1,0,2:T(2,128)(2,1)}), bf16[2,360,5760]{1,0,2:T(2,128)(2,1)}, u32[]{:S(2)}, u32[]{:S(2)}) async-start(bf16[2,360,5760]{1,0,2:T(2,128)(2,1)} %fusion), calls=%async_computation | async-start | bytes 17694720 | tf_op jit(solution)/shard_map/all_to_all | solution.py:29
  93.2 135.7 %all-gather.2.cloned.1.call-start = ((), (), s32[]{:S(2)}) async-start(), calls=%async_computation.1 | async-start | bytes 1554432 | tf_op jit(solution)/shard_map/all_gather | solution.py:23
Sparse Core Ops, SparseCore 0:
  96.8 78.8 all-gather.1
where the time goes:
time: 331 us; the launch traced here: 330 us
  waiting for transfers between devices  103 us (31%)
  local copies, waits for them, and re-layouts  88.8 us (27%)
  blocking collectives  78.6 us (24%)
  other arithmetic  25.2 us (8%)
  between operations  14.1 us (4%)
  matrix products  13.9 us (4%)
  starting transfers between devices  5.53 us (2%)
    all_to_all x1, waiting for transfers between devices, body(): lax.all_to_all(packed, 'col', split_axis=2, concat_axis=1, tiled=True)  103 us
    unnamed x1, blocking collectives  78.6 us
    gather x1, local copies, waits for them, and re-layouts, body(): packed = jnp.take(joined_weight, stored, axis=2)  32 us
    all_to_all x2, local copies, waits for them, and re-layouts, body(): lax.all_to_all(packed, 'col', split_axis=2, concat_axis=1, tiled=True)  25.9 us
    select_n x2, other arithmetic, body(): packed = jnp.take(joined_weight, stored, axis=2)  23.6 us
    unnamed x5, local copies, waits for them, and re-layouts  23.6 us
    dot_general x1, matrix products, body(): jnp.einsum('ntf,nfd->td', active, down_weight, preferred_element_type=jnp...  9.01 us
  transfers between devices with their start and end apart: 2, of which 1 were waited for; matrix products, arithmetic and copies ran while one was open for 5% of the time, Pallas kernels for 0%

commit v1 on v0

v1 whole, which is shorter than its diff:
```python
import functools

import jax
import jax.numpy as jnp
import numpy as np
from jax import lax
from jax.experimental import pallas as pl
from jax.experimental.pallas import tpu as pltpu
from jax.sharding import PartitionSpec as P

MESH = pl.DeviceIdType.MESH
LANES = 128
WINDOW = 256


def partner_of(me, step, size):
    other = me
    bit = 1
    while bit < size:
        other = other + ((step // bit) % 2) * (1 - 2 * ((me // bit) % 2)) * bit
        bit *= 2
    return other


def block_plan(half, tile_cols):
    unit = tile_cols // 2
    plan, rows = [], []
    for first in range(0, half, LANES):
        units = first + np.arange(LANES)
        tiles = sorted(set((units[units < half] // unit).tolist()))
        at = []
        for tile in tiles:
            mine = (units // unit == tile) & (units < half)
            lane = np.where(mine, 2 * (units % unit), -(1 << 20))
            at.append(len(rows))
            rows.append(np.concatenate([lane, lane + 1]))
        plan.append((first, tiles, at))
    return plan, np.stack(rows).astype(np.int32)


def pack_kernel(n, plan, tiles_each, padded, start_ref, off_ref, lane_ref, joined_ref, recv_ref,
                held, send_buf, pick, send_sem, recv_sem, own_sem, load_sem):
    me, row = lax.axis_index("col"), lax.axis_index("row")
    local, blocks = joined_ref.shape[0], held.shape[0]

    def load_of(b):
        return pltpu.make_async_copy(
            joined_ref.at[:, :, b * LANES:(b + 1) * LANES], held.at[b], load_sem.at[b]
        )

    for b in range(blocks):
        load_of(b).start()
    barrier = pltpu.get_barrier_semaphore()
    for step in range(1, n):
        pl.semaphore_signal(barrier, inc=1, device_id=(row, partner_of(me, step, n)), device_id_type=MESH)
    pl.semaphore_wait(barrier, n - 1)

    def copy_of(turn, other):
        return pltpu.make_async_remote_copy(
            src_ref=send_buf.at[turn],
            dst_ref=recv_ref.at[me],
            send_sem=send_sem.at[turn],
            recv_sem=recv_sem.at[turn],
            device_id=(row, other),
            device_id_type=MESH,
        )

    def step_of(turn):
        return (n - 1) - (2 * turn) % (n - 1)

    def pack(turn, other):
        rows = lax.broadcasted_iota(jnp.int32, (WINDOW, 2 * LANES), 0)
        for first, tiles, at in plan:
            starts = []
            for k, tile in enumerate(tiles):
                starts.append(start_ref[other * tiles_each + tile])
                off = off_ref[other * tiles_each + tile]
                wanted = lane_ref[pl.ds(at[k], 1), :] + off
                pick[k * WINDOW:(k + 1) * WINDOW, :] = jnp.where(rows == wanted, 1.0, 0.0).astype(pick.dtype)
            depth = len(tiles) * WINDOW
            for e in range(local):
                x = jnp.concatenate([held[s + w, e] for s in starts for w in range(WINDOW // LANES)], axis=1)
                y = jnp.dot(x, pick[:depth, :], preferred_element_type=jnp.float32).astype(send_buf.dtype)
                send_buf[turn, e, :, first:first + LANES] = y[:, :LANES]
                send_buf[turn, e, :, padded + first:padded + first + LANES] = y[:, LANES:]

    def send(turn, carry):
        other = partner_of(me, step_of(turn), n)
        pack(turn, other)
        copy_of(turn, other).start()
        return carry

    for b in range(blocks):
        load_of(b).wait()
    lax.fori_loop(0, n - 1, send, 0)
    pack(n - 1, me)
    own = pltpu.make_async_copy(send_buf.at[n - 1], recv_ref.at[me], own_sem)
    own.start()

    def finish(turn, carry):
        copy_of(turn, partner_of(me, step_of(turn), n)).wait()
        return carry

    lax.fori_loop(0, n - 1, finish, 0)
    own.wait()


def exchange(joined_weight, start, off, n, half, tile_cols):
    local, rows, width = joined_weight.shape
    plan, lanes = block_plan(half, tile_cols)
    padded = len(plan) * LANES
    most = max(len(tiles) for _, tiles, _ in plan)
    smem = pl.BlockSpec(memory_space=pltpu.SMEM)
    vmem = pl.BlockSpec(memory_space=pltpu.VMEM)
    return pl.pallas_call(
        functools.partial(pack_kernel, n, plan, 2 * half // tile_cols, padded),
        out_shape=jax.ShapeDtypeStruct((n, local, rows, 2 * padded), joined_weight.dtype),
        in_specs=[smem, smem, vmem, pl.BlockSpec(memory_space=pl.ANY)],
        out_specs=pl.BlockSpec(memory_space=pl.ANY),
        scratch_shapes=[
            pltpu.VMEM((width // LANES, local, rows, LANES), joined_weight.dtype),
            pltpu.VMEM((n, local, rows, 2 * padded), joined_weight.dtype),
            pltpu.VMEM((most * WINDOW, 2 * LANES), joined_weight.dtype),
            pltpu.SemaphoreType.DMA((n - 1,)),
            pltpu.SemaphoreType.DMA((n - 1,)),
            pltpu.SemaphoreType.DMA,
            pltpu.SemaphoreType.DMA((width // LANES,)),
        ],
        compiler_params=pltpu.CompilerParams(
            collective_id=0, has_side_effects=True, vmem_limit_bytes=48 << 20
        ),
        cost_estimate=pl.CostEstimate(
            flops=2 * local * rows * WINDOW * 2 * width, bytes_accessed=4 * local * rows * width, transcendentals=0
        ),
        name="exchange",
    )(start, off, jnp.asarray(lanes), joined_weight)


def expert_kernel(n, padded, recv_ref, tok_ref, share_ref, down_ref, gate_ref, up_ref, part_ref, total):
    e, last = pl.program_id(0), pl.num_programs(0) - 1
    rows, half = recv_ref.shape[2], gate_ref.shape[2]
    for c in range(n):
        gate_ref[0, c * rows:(c + 1) * rows, :] = recv_ref[c, 0, :, :half]
        up_ref[0, c * rows:(c + 1) * rows, :] = recv_ref[c, 0, :, padded:padded + half]
    tokens = tok_ref[...]
    pre_gate = jnp.dot(tokens, gate_ref[0], preferred_element_type=jnp.float32)
    pre_up = jnp.dot(tokens, up_ref[0], preferred_element_type=jnp.float32)
    active = share_ref[0] * (pre_up + 1.0) * pre_gate * jax.nn.sigmoid(1.702 * pre_gate)
    active = active.astype(down_ref.dtype)
    depth = down_ref.shape[2]
    for first in range(0, depth, 512):
        cols = slice(first, min(depth, first + 512))
        term = jnp.dot(active, down_ref[0, :, cols], preferred_element_type=jnp.float32)

        @pl.when(e == 0)
        def _():
            total[:, cols] = term

        @pl.when(e > 0)
        def _():
            total[:, cols] += term

    @pl.when(e == last)
    def _():
        part_ref[...] = total[...].astype(part_ref.dtype)


def experts(recv, tokens, share, down_weight):
    n, local, rows, wide = recv.shape
    half, depth = down_weight.shape[1:]
    count = tokens.shape[0]
    dtype = recv.dtype
    return pl.pallas_call(
        functools.partial(expert_kernel, n, wide // 2),
        grid=(local,),
        out_shape=(
            jax.ShapeDtypeStruct((local, n * rows, half), dtype),
            jax.ShapeDtypeStruct((local, n * rows, half), dtype),
            jax.ShapeDtypeStruct((count, depth), dtype),
        ),
        in_specs=[
            pl.BlockSpec((n, 1, rows, wide), lambda e: (0, e, 0, 0)),
            pl.BlockSpec((count, depth), lambda e: (0, 0)),
            pl.BlockSpec((1, count, 1), lambda e: (e, 0, 0)),
            pl.BlockSpec((1, half, depth), lambda e: (e, 0, 0)),
        ],
        out_specs=(
            pl.BlockSpec((1, n * rows, half), lambda e: (e, 0, 0)),
            pl.BlockSpec((1, n * rows, half), lambda e: (e, 0, 0)),
            pl.BlockSpec((count, depth), lambda e: (0, 0)),
        ),
        scratch_shapes=[pltpu.VMEM((count, depth), jnp.float32)],
        compiler_params=pltpu.CompilerParams(
            dimension_semantics=("arbitrary",), vmem_limit_bytes=56 << 20
        ),
        name="experts",
    )(recv, tokens, share, down_weight)


def reduce_kernel(n, m, part_ref, out_ref, near, far, sums, held, near_send, near_recv, far_send, far_recv):
    me, row = lax.axis_index("col"), lax.axis_index("row")
    barrier = pltpu.get_barrier_semaphore()
    for step in range(1, n):
        pl.semaphore_signal(barrier, inc=1, device_id=(row, partner_of(me, step, n)), device_id_type=MESH)
    for step in range(1, m):
        pl.semaphore_signal(barrier, inc=1, device_id=(partner_of(row, step, m), me), device_id_type=MESH)
    pl.semaphore_wait(barrier, n + m - 2)
    slab = part_ref.shape[0] // n
    own = out_ref.shape[0]
    copies = []
    for step in range(n - 1, 0, -1):
        other = partner_of(me, step, n)
        copies.append(pltpu.make_async_remote_copy(
            src_ref=part_ref.at[pl.ds(pl.multiple_of(other * slab, slab), slab)],
            dst_ref=near.at[step - 1],
            send_sem=near_send.at[step - 1],
            recv_sem=near_recv.at[step - 1],
            device_id=(row, other),
            device_id_type=MESH,
        ))
        copies[-1].start()
    for copy in copies:
        copy.wait()
    total = part_ref[pl.ds(pl.multiple_of(me * slab, slab), slab), :].astype(jnp.float32)
    for step in range(1, n):
        total = total + near[step - 1].astype(jnp.float32)
    for r in range(m):
        sums[r] = total[r * own:(r + 1) * own, :]
        held[r] = total[r * own:(r + 1) * own, :].astype(held.dtype)
    copies = []
    for step in range(m - 1, 0, -1):
        other = partner_of(row, step, m)
        copies.append(pltpu.make_async_remote_copy(
            src_ref=held.at[other],
            dst_ref=far.at[step - 1],
            send_sem=far_send.at[step - 1],
            recv_sem=far_recv.at[step - 1],
            device_id=(other, me),
            device_id_type=MESH,
        ))
        copies[-1].start()
    for copy in copies:
        copy.wait()
    total = sums[row]
    for step in range(1, m):
        total = total + far[step - 1].astype(jnp.float32)
    out_ref[...] = total.astype(out_ref.dtype)


def reduce_scatter(part, n, m):
    count, depth = part.shape
    own = count // (n * m)
    vmem = pl.BlockSpec(memory_space=pltpu.VMEM)
    dma = pltpu.SemaphoreType.DMA
    return pl.pallas_call(
        functools.partial(reduce_kernel, n, m),
        out_shape=jax.ShapeDtypeStruct((own, depth), part.dtype),
        in_specs=[vmem],
        out_specs=vmem,
        scratch_shapes=[
            pltpu.VMEM((n - 1, count // n, depth), part.dtype),
            pltpu.VMEM((m - 1, own, depth), part.dtype),
            pltpu.VMEM((m, own, depth), jnp.float32),
            pltpu.VMEM((m, own, depth), part.dtype),
            dma((n - 1,)), dma((n - 1,)), dma((m - 1,)), dma((m - 1,)),
        ],
        compiler_params=pltpu.CompilerParams(
            collective_id=1, has_side_effects=True, vmem_limit_bytes=48 << 20
        ),
        name="reduce_scatter",
    )(part)


def body(joined_weight, tile_perm, down_weight, tokens, expert_ids, route_scores):
    n, m = lax.axis_size("col"), lax.axis_size("row")
    local, _, width = joined_weight.shape
    half = width // 2 // n
    tiles = tile_perm.shape[0]
    tile_cols = width // tiles
    places = jnp.arange(tiles, dtype=jnp.int32)
    inverse = jnp.sum(places[:, None] * (tile_perm[:, None] == places[None, :]), axis=0)
    first = inverse * tile_cols
    block = jnp.minimum(first // LANES, width // LANES - WINDOW // LANES)
    recv = exchange(joined_weight, block, first - block * LANES, n, half, tile_cols)
    everything = lax.all_gather(tokens, ("col", "row"), axis=0, tiled=True)
    expert_global = lax.axis_index("row") * local + jnp.arange(local, dtype=jnp.int32)
    weights = route_scores / jnp.sum(route_scores, axis=1, keepdims=True)
    share = jnp.sum(
        weights[None, :, :] * (expert_ids[None, :, :] == expert_global[:, None, None]), axis=2
    )
    own = tokens.shape[0]
    share = share.reshape(local, m, n, own).transpose(0, 2, 1, 3).reshape(local, -1, 1)
    gate, up, part = experts(recv, everything, share, down_weight)
    return gate, up, reduce_scatter(part, n, m)


def solution(mesh):
    placed = (P("row", "col", None), P(), P("row", "col", None), P(("row", "col"), None), P(), P())
    return jax.shard_map(
        body,
        mesh=mesh,
        in_specs=placed,
        out_specs=(P("row", None, "col"), P("row", None, "col"), P(("row", "col"), None)),
        check_vma=False,
    )
```

time: 331 us -> 185 us (0.56)
  Pallas kernels: 0 us -> 151 us
  waiting for transfers between devices: 103 us -> 0.7 us
  blocking collectives: 78.6 us -> 0 us
  local copies, waits for them, and re-layouts: 88.8 us -> 15.3 us
  other arithmetic: 25.2 us -> 2.97 us
  matrix products: 13.9 us -> 0 us
  starting transfers between devices: 5.53 us -> 0.04 us
    pallas_call x0 -> x3, Pallas kernels: none -> 151 us  [the longest x1 110 us: exchange(): pl.pallas_call(functools.partial(pack_kernel, n, plan, 2 * half // tile_c...]
    all_to_all x1 -> x0, waiting for transfers between devices: 103 us -> none  [body(): lax.all_to_all(packed, 'col', split_axis=2, concat_axis=1, tiled=True)]
    unnamed x1 -> x0, blocking collectives: 78.6 us -> none
    gather x1 -> x0, local copies, waits for them, and re-layouts: 32 us -> none  [body(): packed = jnp.take(joined_weight, stored, axis=2)]
    all_to_all x2 -> x0, local copies, waits for them, and re-layouts: 25.9 us -> none  [body(): lax.all_to_all(packed, 'col', split_axis=2, concat_axis=1, tiled=True)]
    select_n x3 -> x0, other arithmetic: 23.7 us -> none  [the longest x2 23.6 us: body(): packed = jnp.take(joined_weight, stored, axis=2)]
    dot_general x2 -> x0, matrix products: 13.9 us -> none  [the longest x1 9.01 us: body(): jnp.einsum('ntf,nfd->td', active, down_weight, preferred_element_type=jnp...]
    unnamed x5 -> x7, local copies, waits for them, and re-layouts: 23.6 us -> 14.3 us
  transfers between devices with their start and end apart: 2 -> 1, of which waited for: 1 -> 0; matrix products, arithmetic and copies ran while one was open for 5% -> 2% of each run, Pallas kernels for 0% -> 60%
where the time goes in v1:
time: 185 us; the launch traced here: 184 us
  Pallas kernels  151 us (82%)
  local copies, waits for them, and re-layouts  15.3 us (8%)
  between operations  14.1 us (8%)
  other arithmetic  2.97 us (2%)
    pallas_call x1, Pallas kernels, exchange(): pl.pallas_call(functools.partial(pack_kernel, n, plan, 2 * half // tile_c...  110 us
    pallas_call x1, Pallas kernels, reduce_scatter(): pl.pallas_call(functools.partial(reduce_kernel, n, m), out_shape=jax.Shap...  27.4 us
    unnamed x7, local copies, waits for them, and re-layouts  14.3 us
    pallas_call x1, Pallas kernels, experts(): pl.pallas_call(functools.partial(expert_kernel, n, wide // 2), grid=(loca...  13.5 us
  transfers between devices with their start and end apart: 1, of which 0 were waited for; matrix products, arithmetic and copies ran while one was open for 2% of the time, Pallas kernels for 60%

profile of v1, /device:TPU:0, one launch (start us, length us, event | category | flops | bytes accessed | tf_op | source)
XLA Modules:
  0.0 184.1 jit_solution(16941428728453943400)
XLA Ops:
  7.2 0.0 all-gather.2.cloned.1.call-start
  7.2 0.7 all-gather.2.cloned.1.call-update
  7.9 0.7 reduce_sum.28
  8.6 0.7 broadcast_divide_fusion
  9.3 0.8 select_reduce_fusion.1
  10.1 0.1 reshape.20
  10.2 0.8 reshape.22.share_ref
  11.0 0.8 select_reduce_fusion
  11.8 0.0 copy-start.1
  11.8 0.7 copy-done.1
  12.6 110.1 %exchange.1.recv_ref = bf16[8,2,360,768]{3,2,1,0:T(8,128)(2,1)} custom-call(s32[144]{0:T(256)S(1)} %get-tuple-element.19.start_ref, s32[144]{0:T(256)S(1)} %get-tuple-element.18.off_ref, s32[20,256]{1,0:T(8,128)S(1)} %copy-done.1, bf16[2,360,5760]{2,1,0:T(8,128)(2,1)} %joined_ref.1), custom_call_target="tpu_custom_call" | custom-call | flops 4246732800 | bytes 16588800 | tf_op jit(solution)/shard_map/exchange/pallas_call | solution.py:115
  122.7 0.0 all-gather.2.cloned.1.call-done.tok_ref
  122.7 13.5 %experts.1 = (bf16[2,2880,360]{2,1,0:T(8,128)(2,1)}, bf16[2,2880,360]{2,1,0:T(8,128)(2,1)}, bf16[256,2880]{1,0:T(8,128)(2,1)}) custom-call(bf16[8,2,360,768]{3,2,1,0:T(8,128)(2,1)} %exchange.1.recv_ref, bf16[256,2880]{1,0:T(8,128)(2,1)} %all-gather.2.cloned.1.call-done.tok_ref, f32[2,256,1]{2,1,0:T(8,128)} %reshape.22.share_ref, bf16[2,360,2880]{2,1,0:T(8,128)(2,1)} %down_ref.1), custom_call_target="tpu_custom_call" | custom-call | tf_op jit(solution)/shard_map/experts/pallas_call | solution.py:173
  136.3 0.0 copy-start
  136.3 6.5 %copy.22 = bf16[2,2880,360]{1,2,0:T(8,128)(2,1)} copy(bf16[2,2880,360]{2,1,0:T(8,128)(2,1)} %get-tuple-element.15) | data formatting | bytes 8294400
  142.8 0.0 copy-done
  142.8 27.4 %reduce_scatter.1 = bf16[8,2880]{1,0:T(8,128)(2,1)S(1)} custom-call(bf16[256,2880]{1,0:T(8,128)(2,1)S(1)} %copy-done), custom_call_target="tpu_custom_call" | custom-call | tf_op jit(solution)/shard_map/reduce_scatter/pallas_call | solution.py:255
  170.2 6.4 %copy.23 = bf16[2,2880,360]{1,2,0:T(8,128)(2,1)} copy(bf16[2,2880,360]{2,1,0:T(8,128)(2,1)} %get-tuple-element.16) | data formatting | bytes 8294400
  176.7 0.6 copy.25
  (3 shorter events, 0.0 us)
Async XLA Ops:
  7.2 115.6 %all-gather.2.cloned.1.call-start = ((), (), s32[]{:S(2)}) async-start(), calls=%async_computation | async-start | bytes 1554432 | tf_op jit(solution)/shard_map/all_gather | solution.py:285
  11.8 0.7 copy-start.1
  136.3 6.6 %copy-start = (bf16[256,2880]{1,0:T(8,128)(2,1)S(1)}, bf16[256,2880]{1,0:T(8,128)(2,1)}, u32[]{:S(2)}) copy-start(bf16[256,2880]{1,0:T(8,128)(2,1)} %get-tuple-element.8.part_ref) | copy-start | bytes 4423684
Sparse Core Ops, SparseCore 0:
  10.8 99.9 all-gather.1

commit v2 on v1

v2 whole, which is shorter than its diff:
```python
import functools

import jax
import jax.numpy as jnp
import numpy as np
from jax import lax
from jax.experimental import pallas as pl
from jax.experimental.pallas import tpu as pltpu
from jax.sharding import PartitionSpec as P

MESH = pl.DeviceIdType.MESH
LANES = 128
WINDOW = 256
NT = (((1,), (1,)), ((), ()))


def partner_of(me, step, size):
    other = me
    bit = 1
    while bit < size:
        other = other + ((step // bit) % 2) * (1 - 2 * ((me // bit) % 2)) * bit
        bit *= 2
    return other


def block_plan(half, tile_cols):
    unit = tile_cols // 2
    plan, rows = [], []
    for first in range(0, half, LANES):
        units = first + np.arange(LANES)
        tiles = sorted(set((units[units < half] // unit).tolist()))
        at = []
        for tile in tiles:
            mine = (units // unit == tile) & (units < half)
            lane = np.where(mine, 2 * (units % unit), -(1 << 20))
            at.append(len(rows))
            rows.append(np.concatenate([lane, lane + 1]))
        plan.append((first, min(LANES, half - first), tiles, at))
    return plan, np.stack(rows, axis=1).astype(np.int32)


def pack_kernel(n, plan, tiles_each, start_ref, off_ref, lane_ref, joined_ref, recv_ref,
                held, send_buf, pick, send_sem, recv_sem, own_sem, load_sem):
    me, row = lax.axis_index("col"), lax.axis_index("row")
    local, blocks = joined_ref.shape[0], held.shape[0]

    def load_of(b):
        return pltpu.make_async_copy(
            joined_ref.at[:, :, b * LANES:(b + 1) * LANES], held.at[b], load_sem.at[b]
        )

    for b in range(blocks):
        load_of(b).start()
    barrier = pltpu.get_barrier_semaphore()
    for step in range(1, n):
        pl.semaphore_signal(barrier, inc=1, device_id=(row, partner_of(me, step, n)), device_id_type=MESH)
    pl.semaphore_wait(barrier, n - 1)

    def copy_of(turn, other):
        return pltpu.make_async_remote_copy(
            src_ref=send_buf.at[turn],
            dst_ref=recv_ref.at[me],
            send_sem=send_sem.at[turn],
            recv_sem=recv_sem.at[turn],
            device_id=(row, other),
            device_id_type=MESH,
        )

    def step_of(turn):
        return (n - 1) - (2 * turn) % (n - 1)

    def pack(turn, other):
        columns = lax.broadcasted_iota(jnp.int32, (2 * LANES, WINDOW), 1)
        for first, count, tiles, at in plan:
            starts = []
            for k, tile in enumerate(tiles):
                starts.append(start_ref[other * tiles_each + tile])
                off = off_ref[other * tiles_each + tile]
                wanted = lane_ref[:, at[k]:at[k] + 1] + off
                pick[:, k * WINDOW:(k + 1) * WINDOW] = jnp.where(columns == wanted, 1.0, 0.0).astype(pick.dtype)
            depth = len(tiles) * WINDOW
            for e in range(local):
                x = jnp.concatenate([held[s + w, e] for s in starts for w in range(WINDOW // LANES)], axis=1)
                y = lax.dot_general(pick[:, :depth], x, NT, preferred_element_type=jnp.float32)
                y = y.astype(send_buf.dtype)
                send_buf[turn, e, 0, first:first + count, :] = y[:count]
                send_buf[turn, e, 1, first:first + count, :] = y[LANES:LANES + count]

    def send(turn, carry):
        other = partner_of(me, step_of(turn), n)
        pack(turn, other)
        copy_of(turn, other).start()
        return carry

    for b in range(blocks):
        load_of(b).wait()
    lax.fori_loop(0, n - 1, send, 0)
    pack(n - 1, me)
    own = pltpu.make_async_copy(send_buf.at[n - 1], recv_ref.at[me], own_sem)
    own.start()

    def finish(turn, carry):
        copy_of(turn, partner_of(me, step_of(turn), n)).wait()
        return carry

    lax.fori_loop(0, n - 1, finish, 0)
    own.wait()


def exchange(joined_weight, start, off, n, half, tile_cols):
    local, rows, width = joined_weight.shape
    plan, lanes = block_plan(half, tile_cols)
    most = max(len(tiles) for _, _, tiles, _ in plan)
    smem = pl.BlockSpec(memory_space=pltpu.SMEM)
    vmem = pl.BlockSpec(memory_space=pltpu.VMEM)
    return pl.pallas_call(
        functools.partial(pack_kernel, n, plan, 2 * half // tile_cols),
        out_shape=jax.ShapeDtypeStruct((n, local, 2, half, rows), joined_weight.dtype),
        in_specs=[smem, smem, vmem, pl.BlockSpec(memory_space=pl.ANY)],
        out_specs=pl.BlockSpec(memory_space=pl.ANY),
        scratch_shapes=[
            pltpu.VMEM((width // LANES, local, rows, LANES), joined_weight.dtype),
            pltpu.VMEM((n, local, 2, half, rows), joined_weight.dtype),
            pltpu.VMEM((2 * LANES, most * WINDOW), joined_weight.dtype),
            pltpu.SemaphoreType.DMA((n - 1,)),
            pltpu.SemaphoreType.DMA((n - 1,)),
            pltpu.SemaphoreType.DMA,
            pltpu.SemaphoreType.DMA((width // LANES,)),
        ],
        compiler_params=pltpu.CompilerParams(
            collective_id=0, has_side_effects=True, vmem_limit_bytes=48 << 20
        ),
        cost_estimate=pl.CostEstimate(
            flops=2 * local * rows * WINDOW * 2 * width, bytes_accessed=4 * local * rows * width, transcendentals=0
        ),
        name="exchange",
    )(start, off, jnp.asarray(lanes), joined_weight)


def expert_kernel(n, base_ref, recv_ref, tok_ref, ids_ref, scores_ref, order_ref, down_ref,
                  gate_ref, up_ref, part_ref, total):
    e, last = pl.program_id(0), pl.num_programs(0) - 1
    rows = recv_ref.shape[4]
    for c in range(n):
        gate_ref[0, :, c * rows:(c + 1) * rows] = recv_ref[c, 0, 0]
        up_ref[0, :, c * rows:(c + 1) * rows] = recv_ref[c, 0, 1]
    scores = scores_ref[...]
    mine = jnp.where(ids_ref[...] == base_ref[0] + e, scores, 0.0)
    shares = jnp.sum(mine, axis=0, keepdims=True) / jnp.sum(scores, axis=0, keepdims=True)
    count = tok_ref.shape[0]
    source = lax.broadcasted_iota(jnp.int32, (count, count), 1)
    share = jnp.sum(jnp.where(source == order_ref[...], shares, 0.0), axis=1, keepdims=True)
    tokens = tok_ref[...]
    pre_gate = lax.dot_general(tokens, gate_ref[0], NT, preferred_element_type=jnp.float32)
    pre_up = lax.dot_general(tokens, up_ref[0], NT, preferred_element_type=jnp.float32)
    active = share * (pre_up + 1.0) * pre_gate * jax.nn.sigmoid(1.702 * pre_gate)
    active = active.astype(down_ref.dtype)
    depth = down_ref.shape[2]
    for first in range(0, depth, 512):
        cols = slice(first, min(depth, first + 512))
        term = jnp.dot(active, down_ref[0, :, cols], preferred_element_type=jnp.float32)

        @pl.when(e == 0)
        def _():
            total[:, cols] = term

        @pl.when(e > 0)
        def _():
            total[:, cols] += term

    @pl.when(e == last)
    def _():
        part_ref[...] = total[...].astype(part_ref.dtype)


def experts(base, recv, tokens, ids, scores, order, down_weight):
    n, local, _, _, rows = recv.shape
    half, depth = down_weight.shape[1:]
    count = tokens.shape[0]
    dtype = recv.dtype
    return pl.pallas_call(
        functools.partial(expert_kernel, n),
        grid=(local,),
        out_shape=(
            jax.ShapeDtypeStruct((local, half, n * rows), dtype),
            jax.ShapeDtypeStruct((local, half, n * rows), dtype),
            jax.ShapeDtypeStruct((count, depth), dtype),
        ),
        in_specs=[
            pl.BlockSpec(memory_space=pltpu.SMEM),
            pl.BlockSpec((n, 1, 2, half, rows), lambda e: (0, e, 0, 0, 0)),
            pl.BlockSpec((count, depth), lambda e: (0, 0)),
            pl.BlockSpec(ids.shape, lambda e: (0, 0)),
            pl.BlockSpec(scores.shape, lambda e: (0, 0)),
            pl.BlockSpec(order.shape, lambda e: (0, 0)),
            pl.BlockSpec((1, half, depth), lambda e: (e, 0, 0)),
        ],
        out_specs=(
            pl.BlockSpec((1, half, n * rows), lambda e: (e, 0, 0)),
            pl.BlockSpec((1, half, n * rows), lambda e: (e, 0, 0)),
            pl.BlockSpec((count, depth), lambda e: (0, 0)),
        ),
        scratch_shapes=[pltpu.VMEM((count, depth), jnp.float32)],
        compiler_params=pltpu.CompilerParams(
            dimension_semantics=("arbitrary",), vmem_limit_bytes=56 << 20
        ),
        name="experts",
    )(base, recv, tokens, ids, scores, order, down_weight)


def reduce_kernel(n, m, part_ref, out_ref, first, pairs, near, sums, held, far,
                  first_send, first_recv, near_send, near_recv, far_send, far_recv):
    me, row = lax.axis_index("col"), lax.axis_index("row")
    chip, core, chips = me // 2, me % 2, n // 2
    own, depth = out_ref.shape
    barrier = pltpu.get_barrier_semaphore()
    pl.semaphore_signal(barrier, inc=1, device_id=(row, chip * 2 + 1 - core), device_id_type=MESH)
    for step in range(1, chips):
        other = partner_of(chip, step, chips) * 2 + core
        pl.semaphore_signal(barrier, inc=1, device_id=(row, other), device_id_type=MESH)
    for step in range(1, m):
        pl.semaphore_signal(barrier, inc=1, device_id=(partner_of(row, step, m), me), device_id_type=MESH)
    pl.semaphore_wait(barrier, chips + m - 1)

    half = depth // 2 // LANES * LANES
    chunks = [slice(0, half), slice(half, depth)]

    def sibling(at, cols):
        return [pltpu.make_async_remote_copy(
            src_ref=part_ref.at[:, 1 - core, :, cols],
            dst_ref=first.at[:, :, cols],
            send_sem=first_send.at[at],
            recv_sem=first_recv.at[at],
            device_id=(row, chip * 2 + 1 - core),
            device_id_type=MESH,
        )]

    def plane(at, cols):
        copies = []
        for step in range(chips - 1, 0, -1):
            other = partner_of(chip, step, chips)
            copies.append(pltpu.make_async_remote_copy(
                src_ref=pairs.at[other, :, cols],
                dst_ref=near.at[step - 1, :, cols],
                send_sem=near_send.at[at, step - 1],
                recv_sem=near_recv.at[at, step - 1],
                device_id=(row, other * 2 + core),
                device_id_type=MESH,
            ))
        return copies

    def along(at, cols):
        copies = []
        for step in range(m - 1, 0, -1):
            other = partner_of(row, step, m)
            copies.append(pltpu.make_async_remote_copy(
                src_ref=held.at[other, :, cols],
                dst_ref=far.at[step - 1, :, cols],
                send_sem=far_send.at[at, step - 1],
                recv_sem=far_recv.at[at, step - 1],
                device_id=(other, me),
                device_id_type=MESH,
            ))
        return copies

    def start(copies):
        for copy in copies:
            copy.start()

    def wait(copies):
        for copy in copies:
            copy.wait()

    for at, cols in enumerate(chunks):
        start(sibling(at, cols))
    for at, cols in enumerate(chunks):
        wait(sibling(at, cols))
        for q in range(chips):
            both = part_ref[q, core, :, cols].astype(jnp.float32) + first[q, :, cols].astype(jnp.float32)
            pairs[q, :, cols] = both.astype(pairs.dtype)
        start(plane(at, cols))
    for at, cols in enumerate(chunks):
        wait(plane(at, cols))
        total = pairs[chip, :, cols].astype(jnp.float32)
        for step in range(1, chips):
            total = total + near[step - 1, :, cols].astype(jnp.float32)
        for r in range(m):
            sums[r, :, cols] = total[r * own:(r + 1) * own, :]
            held[r, :, cols] = total[r * own:(r + 1) * own, :].astype(held.dtype)
        start(along(at, cols))
    for at, cols in enumerate(chunks):
        wait(along(at, cols))
        total = sums[row, :, cols]
        for step in range(1, m):
            total = total + far[step - 1, :, cols].astype(jnp.float32)
        out_ref[:, cols] = total.astype(out_ref.dtype)


def reduce_scatter(part, n, m):
    count, depth = part.shape
    own, slab, chips = count // (n * m), count // n, n // 2
    vmem = pl.BlockSpec(memory_space=pltpu.VMEM)
    dma = pltpu.SemaphoreType.DMA
    return pl.pallas_call(
        functools.partial(reduce_kernel, n, m),
        out_shape=jax.ShapeDtypeStruct((own, depth), part.dtype),
        in_specs=[vmem],
        out_specs=vmem,
        scratch_shapes=[
            pltpu.VMEM((chips, slab, depth), part.dtype),
            pltpu.VMEM((chips, slab, depth), part.dtype),
            pltpu.VMEM((chips - 1, slab, depth), part.dtype),
            pltpu.VMEM((m, own, depth), jnp.float32),
            pltpu.VMEM((m, own, depth), part.dtype),
            pltpu.VMEM((m - 1, own, depth), part.dtype),
            dma((2,)), dma((2,)), dma((2, chips - 1)), dma((2, chips - 1)), dma((2, m - 1)), dma((2, m - 1)),
        ],
        compiler_params=pltpu.CompilerParams(
            collective_id=1, has_side_effects=True, vmem_limit_bytes=48 << 20
        ),
        name="reduce_scatter",
    )(part.reshape(chips, 2, slab, depth))


def body(joined_weight, tile_perm, down_weight, tokens, expert_ids, route_scores):
    n, m = lax.axis_size("col"), lax.axis_size("row")
    local, _, width = joined_weight.shape
    half = width // 2 // n
    tiles = tile_perm.shape[0]
    tile_cols = width // tiles
    places = jnp.arange(tiles, dtype=jnp.int32)
    inverse = jnp.sum(places[:, None] * (tile_perm[:, None] == places[None, :]), axis=0)
    first = inverse * tile_cols
    block = jnp.minimum(first // LANES, width // LANES - WINDOW // LANES)
    recv = exchange(joined_weight, block, first - block * LANES, n, half, tile_cols)
    everything = lax.all_gather(tokens, ("col", "row"), axis=0, tiled=True)
    base = lax.axis_index("row").astype(jnp.int32).reshape(1) * local
    own = tokens.shape[0]
    order = np.arange(m * n * own, dtype=np.int32).reshape(m, n, own).transpose(1, 0, 2).reshape(-1, 1)
    gate, up, part = experts(
        base, recv, everything, expert_ids.T, route_scores.T, jnp.asarray(order), down_weight
    )
    return jnp.swapaxes(gate, 1, 2), jnp.swapaxes(up, 1, 2), reduce_scatter(part, n, m)


def solution(mesh):
    placed = (P("row", "col", None), P(), P("row", "col", None), P(("row", "col"), None), P(), P())
    return jax.shard_map(
        body,
        mesh=mesh,
        in_specs=placed,
        out_specs=(P("row", None, "col"), P("row", None, "col"), P(("row", "col"), None)),
        check_vma=False,
    )
```

time: 185 us -> 163 us (0.88)
  local copies, waits for them, and re-layouts: 15.3 us -> 2.9 us
  Pallas kernels: 151 us -> 144 us
  other arithmetic: 2.97 us -> 0.79 us
    unnamed x7 -> x5, local copies, waits for them, and re-layouts: 14.3 us -> 2.9 us
    pallas_call x1, Pallas kernels: 27.4 us -> 19.6 us  [reduce_scatter(): pl.pallas_call(functools.partial(reduce_kernel, n, m), out_shape=jax.Shap...]
  transfers between devices with their start and end apart: 1 -> 1, of which waited for: 0 -> 0; matrix products, arithmetic and copies ran while one was open for 2% -> 0% of each run, Pallas kernels for 60% -> 68%
where the time goes in v2:
time: 163 us
  Pallas kernels  144 us (88%)
  between operations  14.1 us (9%)
  local copies, waits for them, and re-layouts  2.9 us (2%)
    pallas_call x1, Pallas kernels, exchange(): pl.pallas_call(functools.partial(pack_kernel, n, plan, 2 * half // tile_c...  111 us
    pallas_call x1, Pallas kernels, reduce_scatter(): pl.pallas_call(functools.partial(reduce_kernel, n, m), out_shape=jax.Shap...  19.6 us
    pallas_call x1, Pallas kernels, experts(): pl.pallas_call(functools.partial(expert_kernel, n), grid=(local,), out_sh...  13.7 us
  transfers between devices with their start and end apart: 1, of which 0 were waited for; matrix products, arithmetic and copies ran while one was open for 0% of the time, Pallas kernels for 68%

profile of v2, /device:TPU:0, one launch (start us, length us, event | category | flops | bytes accessed | tf_op | source)
XLA Modules:
  0.0 162.8 jit_solution(6559228427283579165)
XLA Ops:
  7.2 0.0 all-gather.2.cloned.1.call-start
  7.2 0.7 all-gather.2.cloned.1.call-update
  7.9 0.8 select_reduce_fusion
  8.7 0.0 copy-start.1
  8.7 0.9 copy-done.1
  9.6 111.0 %exchange.1.recv_ref = bf16[8,2,2,360,360]{4,3,2,1,0:T(8,128)(2,1)} custom-call(s32[144]{0:T(256)S(1)} %get-tuple-element.10.start_ref, s32[144]{0:T(256)S(1)} %get-tuple-element.9.off_ref, s32[256,20]{1,0:T(8,128)S(1)} %copy-done.1, bf16[2,360,5760]{2,1,0:T(8,128)(2,1)} %joined_ref.1), custom_call_target="tpu_custom_call" | custom-call | flops 4246732800 | bytes 16588800 | tf_op jit(solution)/shard_map/exchange/pallas_call | solution.py:116
  120.6 0.0 all-gather.2.cloned.1.call-done.tok_ref
  120.7 13.7 %experts.1 = (bf16[2,360,2880]{2,1,0:T(8,128)(2,1)}, bf16[2,360,2880]{2,1,0:T(8,128)(2,1)}, bf16[256,2880]{1,0:T(8,128)(2,1)}) custom-call(s32[1]{0:T(128)} %bitcast.base_ref, bf16[8,2,2,360,360]{4,3,2,1,0:T(8,128)(2,1)} %exchange.1.recv_ref, bf16[256,2880]{1,0:T(8,128)(2,1)} %all-gather.2.cloned.1.call-done.tok_ref, s32[4,256]{1,0:T(4,128)} %bitcast.7, ...), custom_call_target="tpu_custom_call" | custom-call | tf_op jit(solution)/shard_map/experts/pallas_call | solution.py:181
  134.4 0.0 copy-start
  134.4 1.4 copy-done
  135.7 19.6 %reduce_scatter.1 = bf16[8,2880]{1,0:T(8,128)(2,1)S(1)} custom-call(bf16[4,2,32,2880]{3,2,1,0:T(8,128)(2,1)S(1)} %bitcast.6), custom_call_target="tpu_custom_call" | custom-call | tf_op jit(solution)/shard_map/reduce_scatter/pallas_call | solution.py:304
  155.3 0.6 copy.12
  (1 shorter events, 0.0 us)
Async XLA Ops:
  7.2 113.5 %all-gather.2.cloned.1.call-start = ((), (), s32[]{:S(2)}) async-start(), calls=%async_computation | async-start | bytes 1554432 | tf_op jit(solution)/shard_map/all_gather | solution.py:336
  8.7 0.9 copy-start.1
  134.4 1.4 copy-start
Sparse Core Ops, SparseCore 0:
  10.8 97.8 all-gather.1

commit v3 on v2

--- a/solution.py
+++ b/solution.py
@@ -138,12 +138,17 @@
 
 
 def expert_kernel(n, base_ref, recv_ref, tok_ref, ids_ref, scores_ref, order_ref, down_ref,
-                  gate_ref, up_ref, part_ref, total):
-    e, last = pl.program_id(0), pl.num_programs(0) - 1
-    rows = recv_ref.shape[4]
+                  gate_ref, up_ref, part_ref, total, both):
+    e, part = pl.program_id(0), pl.program_id(1)
+    begin = (e == 0) & (part == 0)
+    last = (e == pl.num_programs(0) - 1) & (part == pl.num_programs(1) - 1)
+    units, rows = recv_ref.shape[3:]
+    second = both.shape[0] // 2
     for c in range(n):
-        gate_ref[0, :, c * rows:(c + 1) * rows] = recv_ref[c, 0, 0]
-        up_ref[0, :, c * rows:(c + 1) * rows] = recv_ref[c, 0, 1]
+        both[:units, c * rows:(c + 1) * rows] = recv_ref[c, 0, 0]
+        both[second:second + units, c * rows:(c + 1) * rows] = recv_ref[c, 0, 1]
+    gate_ref[0] = both[:units, :]
+    up_ref[0] = both[second:second + units, :]
     scores = scores_ref[...]
     mine = jnp.where(ids_ref[...] == base_ref[0] + e, scores, 0.0)
     shares = jnp.sum(mine, axis=0, keepdims=True) / jnp.sum(scores, axis=0, keepdims=True)
@@ -151,8 +156,8 @@
     source = lax.broadcasted_iota(jnp.int32, (count, count), 1)
     share = jnp.sum(jnp.where(source == order_ref[...], shares, 0.0), axis=1, keepdims=True)
     tokens = tok_ref[...]
-    pre_gate = lax.dot_general(tokens, gate_ref[0], NT, preferred_element_type=jnp.float32)
-    pre_up = lax.dot_general(tokens, up_ref[0], NT, preferred_element_type=jnp.float32)
+    pre = lax.dot_general(tokens, both[...], NT, preferred_element_type=jnp.float32)
+    pre_gate, pre_up = pre[:, :units], pre[:, second:second + units]
     active = share * (pre_up + 1.0) * pre_gate * jax.nn.sigmoid(1.702 * pre_gate)
     active = active.astype(down_ref.dtype)
     depth = down_ref.shape[2]
@@ -160,15 +165,15 @@
         cols = slice(first, min(depth, first + 512))
         term = jnp.dot(active, down_ref[0, :, cols], preferred_element_type=jnp.float32)
 
-        @pl.when(e == 0)
+        @pl.when(begin)
         def _():
             total[:, cols] = term
 
-        @pl.when(e > 0)
+        @pl.when(jnp.logical_not(begin))
         def _():
             total[:, cols] += term
 
-    @pl.when(e == last)
+    @pl.when(last)
     def _():
         part_ref[...] = total[...].astype(part_ref.dtype)
 
@@ -178,9 +183,11 @@
     half, depth = down_weight.shape[1:]
     count = tokens.shape[0]
     dtype = recv.dtype
+    parts = 3 if half % 24 == 0 else 1
+    units = half // parts
     return pl.pallas_call(
         functools.partial(expert_kernel, n),
-        grid=(local,),
+        grid=(local, parts),
         out_shape=(
             jax.ShapeDtypeStruct((local, half, n * rows), dtype),
             jax.ShapeDtypeStruct((local, half, n * rows), dtype),
@@ -188,21 +195,24 @@
         ),
         in_specs=[
             pl.BlockSpec(memory_space=pltpu.SMEM),
-            pl.BlockSpec((n, 1, 2, half, rows), lambda e: (0, e, 0, 0, 0)),
-            pl.BlockSpec((count, depth), lambda e: (0, 0)),
-            pl.BlockSpec(ids.shape, lambda e: (0, 0)),
-            pl.BlockSpec(scores.shape, lambda e: (0, 0)),
-            pl.BlockSpec(order.shape, lambda e: (0, 0)),
-            pl.BlockSpec((1, half, depth), lambda e: (e, 0, 0)),
+            pl.BlockSpec((n, 1, 2, units, rows), lambda e, p: (0, e, 0, p, 0)),
+            pl.BlockSpec((count, depth), lambda e, p: (0, 0)),
+            pl.BlockSpec(ids.shape, lambda e, p: (0, 0)),
+            pl.BlockSpec(scores.shape, lambda e, p: (0, 0)),
+            pl.BlockSpec(order.shape, lambda e, p: (0, 0)),
+            pl.BlockSpec((1, units, depth), lambda e, p: (e, p, 0)),
         ],
         out_specs=(
-            pl.BlockSpec((1, half, n * rows), lambda e: (e, 0, 0)),
-            pl.BlockSpec((1, half, n * rows), lambda e: (e, 0, 0)),
-            pl.BlockSpec((count, depth), lambda e: (0, 0)),
-        ),
-        scratch_shapes=[pltpu.VMEM((count, depth), jnp.float32)],
+            pl.BlockSpec((1, units, n * rows), lambda e, p: (e, p, 0)),
+            pl.BlockSpec((1, units, n * rows), lambda e, p: (e, p, 0)),
+            pl.BlockSpec((count, depth), lambda e, p: (0, 0)),
+        ),
+        scratch_shapes=[
+            pltpu.VMEM((count, depth), jnp.float32),
+            pltpu.VMEM((2 * (-(-units // LANES) * LANES), n * rows), dtype),
+        ],
         compiler_params=pltpu.CompilerParams(
-            dimension_semantics=("arbitrary",), vmem_limit_bytes=56 << 20
+            dimension_semantics=("arbitrary", "arbitrary"), vmem_limit_bytes=56 << 20
         ),
         name="experts",
     )(base, recv, tokens, ids, scores, order, down_weight)

time: 163 us -> 171 us (1.049)
  Pallas kernels: 144 us -> 152 us
    pallas_call x1, Pallas kernels: 13.7 us -> 21.6 us  [experts(): pl.pallas_call(functools.partial(expert_kernel, n), grid=(local, parts),...]
  transfers between devices with their start and end apart: 1 -> 1, of which waited for: 0 -> 0; matrix products, arithmetic and copies ran while one was open for 0% -> 0% of each run, Pallas kernels for 68% -> 65%
where the time goes in v3:
time: 171 us
  Pallas kernels  152 us (89%)
  between operations  14.1 us (8%)
  local copies, waits for them, and re-layouts  2.9 us (2%)
    pallas_call x1, Pallas kernels, exchange(): pl.pallas_call(functools.partial(pack_kernel, n, plan, 2 * half // tile_c...  111 us
    pallas_call x1, Pallas kernels, experts(): pl.pallas_call(functools.partial(expert_kernel, n), grid=(local, parts),...  21.6 us
    pallas_call x1, Pallas kernels, reduce_scatter(): pl.pallas_call(functools.partial(reduce_kernel, n, m), out_shape=jax.Shap...  19.6 us
  transfers between devices with their start and end apart: 1, of which 0 were waited for; matrix products, arithmetic and copies ran while one was open for 0% of the time, Pallas kernels for 65%

profile of v3, /device:TPU:0, one launch (start us, length us, event | category | flops | bytes accessed | tf_op | source)
XLA Modules:
  0.0 170.7 jit_solution(16466216939299476370)
XLA Ops:
  7.2 0.0 all-gather.2.cloned.1.call-start
  7.2 0.7 all-gather.2.cloned.1.call-update
  7.9 0.8 select_reduce_fusion
  8.7 0.0 copy-start.1
  8.7 0.9 copy-done.1
  9.6 111.0 %exchange.1.recv_ref = bf16[8,2,2,360,360]{4,3,2,1,0:T(8,128)(2,1)} custom-call(s32[144]{0:T(256)S(1)} %get-tuple-element.10.start_ref, s32[144]{0:T(256)S(1)} %get-tuple-element.9.off_ref, s32[256,20]{1,0:T(8,128)S(1)} %copy-done.1, bf16[2,360,5760]{2,1,0:T(8,128)(2,1)} %joined_ref.1), custom_call_target="tpu_custom_call" | custom-call | flops 4246732800 | bytes 16588800 | tf_op jit(solution)/shard_map/exchange/pallas_call | solution.py:116
  120.6 0.0 all-gather.2.cloned.1.call-done.tok_ref
  120.6 21.6 %experts.1 = (bf16[2,360,2880]{2,1,0:T(8,128)(2,1)}, bf16[2,360,2880]{2,1,0:T(8,128)(2,1)}, bf16[256,2880]{1,0:T(8,128)(2,1)}) custom-call(s32[1]{0:T(128)} %bitcast.base_ref, bf16[8,2,2,360,360]{4,3,2,1,0:T(8,128)(2,1)} %exchange.1.recv_ref, bf16[256,2880]{1,0:T(8,128)(2,1)} %all-gather.2.cloned.1.call-done.tok_ref, s32[4,256]{1,0:T(4,128)} %bitcast.7, ...), custom_call_target="tpu_custom_call" | custom-call | tf_op jit(solution)/shard_map/experts/pallas_call | solution.py:188
  142.3 0.0 copy-start
  142.3 1.4 copy-done
  143.6 19.6 %reduce_scatter.1 = bf16[8,2880]{1,0:T(8,128)(2,1)S(1)} custom-call(bf16[4,2,32,2880]{3,2,1,0:T(8,128)(2,1)S(1)} %bitcast.6), custom_call_target="tpu_custom_call" | custom-call | tf_op jit(solution)/shard_map/reduce_scatter/pallas_call | solution.py:314
  163.2 0.6 copy.12
  (1 shorter events, 0.0 us)
Async XLA Ops:
  7.2 113.5 %all-gather.2.cloned.1.call-start = ((), (), s32[]{:S(2)}) async-start(), calls=%async_computation | async-start | bytes 1554432 | tf_op jit(solution)/shard_map/all_gather | solution.py:346
  8.7 0.9 copy-start.1
  142.3 1.4 copy-start
Sparse Core Ops, SparseCore 0:
  10.8 97.8 all-gather.1
